TPU v7x, 32 devices: a whole 2x2x4 slice. The times are simulated.
32 devices in a mesh: dp: 4 (over y, x), ctx: 2 (over core), mp: 4 (over z).
Axes of the slice: x: 2, y: 2, z: 4, core: 2. Of those that a mesh axis runs over, the one named last changes fastest.
Arguments:
- queries: bfloat16 [8192, 2048], P(('dp', 'ctx'), 'mp'), parts along dimension 0, may hold values from -6 to 6
- keys: bfloat16 [8192, 2048], P(('dp', 'ctx'), 'mp'), parts along dimension 0, may hold values from -6 to 6
- values: bfloat16 [8192, 2048], P(('dp', 'ctx'), 'mp'), parts along dimension 0, may hold values from -6 to 6
- segment_ids: int32 [8192], P(('dp', 'ctx')), parts along dimension 0, may hold values from 0 to 5, never falling along the last dimension, each value on 1 to 1024 neighbouring positions
- norm_gain: float32 [2048], P('mp'), may hold values from 0.5 to 1.5
- out_weight: bfloat16 [2048, 4096], P(None, 'mp'), may hold values from -0.125 to 0.125
Outputs:
- projected: bfloat16 [8192, 4096], P(('dp', 'ctx'), 'mp'), parts along dimension 0
There are 4 independent parts, one for each index of `dp`. A program takes and returns all parts, laid end to end along the dimension named above; an argument that names none is the same for every part. Nothing has to cross between parts.
Inputs may be any that keep to these rules, and one draw needn't show every extreme that they name: `segment_ids`: ids never fall along the stream; 6 segments, each of 1 to 1024 consecutive positions, one of exactly 1024.
All inputs are finite; a program needn't handle non-finite values.
Results may differ from a plain program's by a relative error of at most 0.0053.
Values may be sent and summed in bfloat16 or wider, within the bound.
A program may use at most 64 MiB of HBM per device.

v0:
```python
import jax
import jax.numpy as jnp
from jax import lax
from jax.sharding import PartitionSpec as P

HEAD = 128


def carried_in(value, axis, join, neutral):
    count, mine = (lax.axis_size(axis), lax.axis_index(axis))
    pieces = jax.tree.map(lambda part: lax.all_gather(part, axis), value)
    so_far = jax.tree.map(
        lambda part, zero: jnp.full_like(part, 0) + jnp.asarray(zero, part.dtype), value, neutral
    )

    def step(position, so_far):
        longer = join(so_far, jax.tree.map(lambda part: part[position], pieces))
        return jax.tree.map(lambda new, old: jnp.where(position < mine, new, old), longer, so_far)

    return lax.fori_loop(0, count - 1, step, so_far)


def features(raw_input):
    return (jax.nn.elu(raw_input.astype(jnp.float32)) + 1.0).astype(jnp.bfloat16)


def join_states(earlier, later):
    early_sum, early_seg = earlier
    later_sum, later_seg = later
    is_blank = later_seg < 0
    linked = early_seg == later_seg
    joined = later_sum + jnp.where(linked, early_sum, 0.0)
    return (jnp.where(is_blank, early_sum, joined), jnp.where(is_blank, early_seg, later_seg))


def per_device(queries, keys, values, segment_ids, norm_gain, out_weight):
    rows_here = queries.shape[0]
    width_here = queries.shape[1]
    heads_here = width_here // HEAD
    feat_query = features(queries).reshape(rows_here, heads_here, HEAD)
    feat_key = features(keys).reshape(rows_here, heads_here, HEAD)
    value_heads = values.reshape(rows_here, heads_here, HEAD)
    final_seg = segment_ids[rows_here - 1]
    in_final = (segment_ids == final_seg).astype(jnp.bfloat16)
    local_sum = jnp.einsum(
        "thd,the->hde",
        feat_key * in_final[:, None, None],
        value_heads,
        preferred_element_type=jnp.float32,
    )
    blank_sum = jnp.zeros_like(local_sum)
    before_sum, before_seg = carried_in(
        (local_sum, final_seg), "ctx", join_states, (blank_sum, jnp.int32(-1))
    )
    position = jnp.arange(rows_here)
    allowed = (position[None, :] <= position[:, None]) & (
        segment_ids[:, None] == segment_ids[None, :]
    )
    scores = jnp.einsum("thd,shd->hts", feat_query, feat_key, preferred_element_type=jnp.float32)
    weights = jnp.where(allowed[None], scores, 0.0).astype(jnp.bfloat16)
    inside = jnp.einsum("hts,she->the", weights, value_heads, preferred_element_type=jnp.float32)
    state_hi = before_sum.astype(jnp.bfloat16)
    state_lo = (before_sum - state_hi.astype(jnp.float32)).astype(jnp.bfloat16)
    carried = jnp.einsum(
        "thd,hde->the", feat_query, state_hi, preferred_element_type=jnp.float32
    ) + jnp.einsum("thd,hde->the", feat_query, state_lo, preferred_element_type=jnp.float32)
    carry_on = (segment_ids == before_seg).astype(jnp.float32)
    numerator = inside + carry_on[:, None, None] * carried
    normed = numerator * lax.rsqrt(jnp.mean(numerator * numerator, axis=-1, keepdims=True) + 1e-06)
    gain_heads = norm_gain.reshape(heads_here, HEAD)
    hidden = (normed * gain_heads[None]).astype(jnp.bfloat16).reshape(rows_here, width_here)
    projected = jnp.dot(
        lax.all_gather(hidden, "mp", axis=1, tiled=True),
        out_weight,
        preferred_element_type=jnp.float32,
    )
    return projected.astype(jnp.bfloat16)


def solution(mesh):
    in_specs = (
        P(("dp", "ctx"), "mp"),
        P(("dp", "ctx"), "mp"),
        P(("dp", "ctx"), "mp"),
        P(("dp", "ctx")),
        P("mp"),
        P(None, "mp"),
    )
    out_specs = P(("dp", "ctx"), "mp")
    return jax.shard_map(
        per_device, mesh=mesh, in_specs=in_specs, out_specs=out_specs, check_vma=False
    )
```

profile of v0, /device:TPU:0, one launch (start us, length us, event | category | flops | bytes accessed | tf_op | source)
XLA Modules:
  0.0 132.4 jit_solution(4126291224746785385)
XLA Ops:
  6.5 0.0 copy-start
  6.5 0.0 all-gather.3.cloned.1.call-start
  6.5 2.4 %fusion = pred[1024,1024]{1,0:T(8,128)(4,1)} fusion(s32[1024]{0:T(1024)} %param.9), kind=kLoop, calls=%fused_computation.6 | loop fusion | flops 3145728 | bytes 1052672 | tf_op jit(solution)/shard_map/and | solution.py:56
  8.9 1.2 dynamic-slice
  10.1 2.0 %slice_dynamic-update-slice_fusion = (s32[2]{0:T(128)S(1)}, s32[1]{0:T(128)}) fusion(s32[2]{0:T(128)S(1)} %broadcast.65, u32[]{:T(128)} %bitcast.2, s32[1024]{0:T(1024)} %param.9), kind=kLoop, calls=%fused_computation.48 | loop fusion | bytes 20
  12.1 1.9 %all-reduce = s32[2]{0:T(128)S(1)} all-reduce(s32[2]{0:T(128)S(1)} %get-tuple-element.19), channel_id=1, replica_groups=mesh['dp'=4,'ctx'=2,'mp'=4] {'ctx'}, use_global_device_ids=true, to_apply=%add | all-reduce | flops 2 | bytes 16
  14.1 0.0 copy-start.3
  14.1 2.2 %fusion.6 = bf16[1024,512]{1,0:T(8,128)(2,1)S(1)} fusion(bf16[1024,512]{1,0:T(8,128)(2,1)} %param.7), kind=kLoop, calls=%fused_computation.12 | loop fusion | flops 3145728 | bytes 2097152 | tf_op jit(solution)/shard_map/convert_element_type | solution.py:24
  16.3 0.5 copy.20
  16.8 0.0 copy-start.2
  16.9 0.0 copy-done.3
  16.9 0.6 compare_convert_fusion.1
  17.5 0.0 copy-done
  17.5 0.4 fusion.10
  18.0 2.4 %all-gather = f32[8,128,128]{2,1,0:T(8,128)S(1)} all-gather(f32[4,128,128]{2,1,0:T(8,128)S(1)} %fusion.10), channel_id=2, replica_groups=mesh['dp'=4,'ctx'=2,'mp'=4] {'ctx'}, dimensions={0}, use_global_device_ids=true | all-gather | bytes 786432 | tf_op jit(solution)/shard_map/all_gather | solution.py:11
  20.3 0.0 copy-done.2
  20.4 0.1 copy.21
  20.5 6.9 %fusion.7 = f32[4,1024,128]{1,2,0:T(8,128)S(1)} fusion(bf16[1024,4,128]{0,2,1:T(8,128)(2,1)} %bitcast.47, pred[1024,1024]{1,0:T(8,128)(4,1)} %fusion, bf16[1024,512]{1,0:T(8,128)(2,1)S(1)} %copy-done, bf16[1024,512]{1,0:T(8,128)(2,1)} %param.6), kind=kOutput, calls=%fused_computation.16 | convolution fusion | flops 2159017984 | bytes 6291456 | tf_op jit(solution)/shard_map/hts,she->the/dot_general | solution.py:61
  27.4 0.0 copy-start.1
  27.4 2.5 %fusion.15 = f32[4,128,1024]{2,1,0:T(8,128)S(1)} fusion(f32[4,128,128]{1,2,0:T(8,128)S(1)} %copy.21, pred[]{:T(512)S(6)} %lt.13, pred[]{:T(512)S(6)} %lt.14, bf16[1024,512]{1,0:T(8,128)(2,1)} %param.6), kind=kOutput, calls=%fused_computation.24 | convolution fusion | flops 137494528 | bytes 3407874 | tf_op jit(solution)/shard_map/thd,hde->the/dot_general | solution.py:64
  29.9 0.0 copy-done.1
  30.0 0.0 copy-start.4
  30.0 1.4 %multiply_reduce_fusion = (f32[1024,4]{0,1:T(4,128)S(1)}, f32[1024,4,128]{0,2,1:T(8,128)S(1)}) fusion(f32[4,128,1024]{2,1,0:T(8,128)S(1)} %fusion.15, f32[4,128,128]{1,2,0:T(8,128)S(1)} %copy.21, pred[]{:T(512)S(6)} %lt.13, pred[]{:T(512)S(6)} %lt.14, f32[1024]{0:T(1024)S(1)} %get-tuple-element.17, f32[4,1024,128]{1,2,0:T(8,128)S(1)} %fusion.7, ...), kind=kOutput, calls=%fused_computation.15 | convolution fusion | flops 140374016 | bytes 7622658 | tf_op jit(solution)/shard_map/thd,hde->the/dot_general | solution.py:66
  31.4 0.0 copy-done.4
  31.4 1.2 multiply_convert_fusion
  32.7 0.0 all-gather.3.cloned.1.call-update
  32.7 83.5 %all-gather.3.cloned.1.call-done = bf16[1024,2048]{0,1:T(8,128)(2,1)} async-done(((bf16[1024,512]{0,1:T(8,128)(2,1)}), bf16[1024,2048]{0,1:T(8,128)(2,1)}) %all-gather.3.cloned.1.call-update) | async-done | bytes 4194320 | tf_op jit(solution)/shard_map/all_gather | solution.py:73
  116.2 9.4 %convolution_convert_fusion = bf16[1024,1024]{1,0:T(8,128)(2,1)} fusion(bf16[1024,2048]{0,1:T(8,128)(2,1)} %all-gather.3.cloned.1.call-done, bf16[2048,1024]{1,0:T(8,128)(2,1)} %param.11), kind=kOutput, calls=%fused_computation.17 | convolution fusion | flops 4296015872 | bytes 10485760 | tf_op jit(solution)/shard_map/dot_general | solution.py:72
  (3 shorter events, 0.0 us)
Async XLA Ops:
  6.5 11.0 %copy-start = (bf16[1024,512]{1,0:T(8,128)(2,1)S(1)}, bf16[1024,512]{1,0:T(8,128)(2,1)}, u32[]{:S(2)}) copy-start(bf16[1024,512]{1,0:T(8,128)(2,1)} %param.8) | copy-start | bytes 3145732
  6.5 109.7 %all-gather.3.cloned.1.call-start = ((), (), s32[]{:S(2)}) async-start(), calls=%async_computation | async-start | bytes 5242880 | tf_op jit(solution)/shard_map/all_gather | solution.py:73
  14.1 2.8 %copy-start.3 = (s32[1024]{0:T(1024)S(1)}, s32[1024]{0:T(1024)}, u32[]{:S(2)}) copy-start(s32[1024]{0:T(1024)} %param.9) | copy-start | bytes 12292
  16.8 3.5 %copy-start.2 = (bf16[1024,512]{0,1:T(8,128)(2,1)}, bf16[1024,512]{0,1:T(8,128)(2,1)S(1)}, u32[]{:S(2)}) copy-start(bf16[1024,512]{0,1:T(8,128)(2,1)S(1)} %copy.20) | copy-start | bytes 3145732
  27.4 2.5 %copy-start.1 = (bf16[1024,512]{1,0:T(8,128)(2,1)S(1)}, bf16[1024,512]{1,0:T(8,128)(2,1)}, u32[]{:S(2)}) copy-start(bf16[1024,512]{1,0:T(8,128)(2,1)} %param.6) | copy-start | bytes 3145732
  30.0 1.5 %copy-start.4 = (f32[512]{0:T(512)S(1)}, f32[512]{0:T(512)}, u32[]{:S(2)}) copy-start(f32[512]{0:T(512)} %param.10) | copy-start | bytes 6148
Sparse Core Ops, SparseCore 0:
  32.8 83.3 all-gather.2
where the time goes:
time: 133 us; the launch traced here: 132 us
  waiting for transfers between devices  83.5 us (63%)
  matrix products  20.7 us (16%)
  between operations  13.6 us (10%)
  other arithmetic  6.4 us (5%)
  blocking collectives  4.28 us (3%)
  local copies, waits for them, and re-layouts  3.94 us (3%)
    all_gather x1, waiting for transfers between devices, per_device(): lax.all_gather(hidden, 'mp', axis=1, tiled=True)  83.5 us
    dot_general x1, matrix products, per_device(): jnp.dot(lax.all_gather(hidden, 'mp', axis=1, tiled=True), out_weight, pre...  9.36 us
    dot_general x1, matrix products, per_device(): jnp.einsum('hts,she->the', weights, value_heads, preferred_element_type=j...  6.93 us
    unnamed x14, local copies, waits for them, and re-layouts  3.38 us
  transfers between devices with their start and end apart: 1, of which 1 were waited for; matrix products, arithmetic and copies ran while one was open for 0% of the time, Pallas kernels for 0%

commit v1 on v0

v1 whole, which is shorter than its diff:
```python
import functools

import jax
import jax.numpy as jnp
from jax import lax
from jax.experimental import pallas as pl
from jax.experimental.pallas import tpu as pltpu
from jax.sharding import PartitionSpec as P

HEAD = 128
MESH = pl.DeviceIdType.MESH
F32, BF16 = jnp.float32, jnp.bfloat16


def features(raw):
    x = raw.astype(F32)
    return jnp.where(x > 0, x + 1.0, jnp.exp(jnp.minimum(x, 0.0))).astype(BF16)


def nn(a, b):
    return lax.dot_general(a, b, (((1,), (0,)), ((), ())), preferred_element_type=F32)


def nt(a, b):
    return lax.dot_general(a, b, (((1,), (1,)), ((), ())), preferred_element_type=F32)


def tn(a, b):
    return lax.dot_general(a, b, (((0,), (0,)), ((), ())), preferred_element_type=F32)


def kernel(n_ctx, n_mp, chunk, q_hbm, k_hbm, v_hbm, seg_ref, gain_ref, w_hbm, out_hbm,
           q, k, v, w, seg_col, mask, state, carry, hid, out_buf,
           load_sem, out_sem, st_send, st_recv, h_send, h_recv):
    ctx, mp = lax.axis_index("ctx"), lax.axis_index("mp")
    rows, width = q.shape
    heads = width // HEAD
    n_chunk = rows // chunk
    loads = []
    for i, (src, dst) in enumerate(((k_hbm, k), (v_hbm, v), (q_hbm, q), (w_hbm, w))):
        c = pltpu.make_async_copy(src, dst, load_sem.at[i])
        c.start()
        loads.append(c)
    barrier = pltpu.get_barrier_semaphore()
    for d in range(1, n_mp):
        pl.semaphore_signal(barrier, inc=1, device_id={"mp": lax.rem(mp + d, n_mp)}, device_id_type=MESH)
    for d in range(1, n_ctx):
        pl.semaphore_signal(barrier, inc=1, device_id={"ctx": lax.rem(ctx + d, n_ctx)}, device_id_type=MESH)

    seg_row = seg_ref[...].astype(F32)
    seg_col[...] = jnp.transpose(jnp.broadcast_to(seg_row, (HEAD, rows)))
    first = seg_col[0:1, :]
    last = seg_col[rows - 1:rows, :]
    in_final = (seg_col[...] == last).astype(BF16)

    loads[0].wait()
    k[...] = features(k[...])
    loads[1].wait()
    for h in range(heads):
        cols = slice(h * HEAD, (h + 1) * HEAD)
        state[ctx, h * HEAD:(h + 1) * HEAD, :] = tn(k[:, cols] * in_final, v[:, cols])
    state[ctx, width:width + 8, :] = jnp.broadcast_to(last, (8, HEAD))
    pl.semaphore_wait(barrier, n_mp - 1 + n_ctx - 1)
    st_copies = []
    for d in range(1, n_ctx):
        c = pltpu.make_async_remote_copy(
            src_ref=state.at[ctx], dst_ref=state.at[ctx], send_sem=st_send.at[d - 1], recv_sem=st_recv.at[d - 1],
            device_id={"ctx": lax.rem(ctx + d, n_ctx)}, device_id_type=MESH)
        c.start()
        st_copies.append(c)

    for i in range(n_chunk):
        r0, r1 = i * chunk, (i + 1) * chunk
        for j in range(r1 // HEAD):
            s0 = j * HEAD
            t = lax.broadcasted_iota(jnp.int32, (chunk, HEAD), 0) + r0
            s = lax.broadcasted_iota(jnp.int32, (chunk, HEAD), 1) + s0
            same = seg_col[r0:r1, :] == seg_row[:, s0:s0 + HEAD]
            mask[r0:r1, s0:s0 + HEAD] = jnp.where(same & (s <= t), 1.0, 0.0).astype(BF16)
    loads[2].wait()
    q[...] = features(q[...])

    for c in st_copies:
        c.wait()
    total = jnp.zeros((width, HEAD), F32)
    for j in range(n_ctx):
        link = (state[j, width:width + 1, :] == first).astype(F32) * (j < ctx).astype(F32)
        total = total + state[j, 0:width, :] * link
    hi = total.astype(BF16)
    carry[:, 0:HEAD] = hi
    carry[:, HEAD:2 * HEAD] = (total - hi.astype(F32)).astype(BF16)

    h_copies = []
    for i in range(n_chunk):
        r0, r1 = i * chunk, (i + 1) * chunk
        on = (seg_col[r0:r1, :] == first).astype(F32)
        for h in range(heads):
            cols = slice(h * HEAD, (h + 1) * HEAD)
            fq = q[r0:r1, cols]
            score = nt(fq, k[0:r1, cols]).astype(BF16) * mask[r0:r1, 0:r1]
            inside = nn(score, v[0:r1, cols])
            both = nn(fq, carry[cols, :])
            numer = inside + on * (both[:, 0:HEAD] + both[:, HEAD:2 * HEAD])
            mean = jnp.mean(numer * numer, axis=-1, keepdims=True)
            hid[mp, r0:r1, cols] = (numer * lax.rsqrt(mean + 1e-6) * gain_ref[:, cols]).astype(BF16)
        for d in range(1, n_mp):
            c = pltpu.make_async_remote_copy(
                src_ref=hid.at[mp, pl.ds(r0, chunk)], dst_ref=hid.at[mp, pl.ds(r0, chunk)],
                send_sem=h_send.at[d - 1, i], recv_sem=h_recv.at[d - 1, i],
                device_id={"mp": lax.rem(mp + d, n_mp)}, device_id_type=MESH)
            c.start()
            h_copies.append(c)

    loads[3].wait()
    outs = []
    for i in range(n_chunk):
        r0, r1 = i * chunk, (i + 1) * chunk
        for d in range(1, n_mp):
            h_copies[i * (n_mp - 1) + d - 1].wait_recv()
        acc = nn(hid[0, r0:r1, :], w[0:width, :])
        for p in range(1, n_mp):
            acc = acc + nn(hid[p, r0:r1, :], w[p * width:(p + 1) * width, :])
        out_buf[r0:r1, :] = acc.astype(BF16)
        c = pltpu.make_async_copy(out_buf.at[pl.ds(r0, chunk)], out_hbm.at[pl.ds(r0, chunk)], out_sem.at[i])
        c.start()
        outs.append(c)
    for c in h_copies:
        c.wait_send()
    for c in outs:
        c.wait()


def per_device(queries, keys, values, segment_ids, norm_gain, out_weight):
    n_ctx, n_mp = lax.axis_size("ctx"), lax.axis_size("mp")
    rows, width = queries.shape
    cols = out_weight.shape[1]
    chunk = 256
    n_chunk = rows // chunk
    any_spec = pl.BlockSpec(memory_space=pl.ANY)
    vmem_spec = pl.BlockSpec(memory_space=pltpu.VMEM)
    dma = pltpu.SemaphoreType.DMA
    return pl.pallas_call(
        functools.partial(kernel, n_ctx, n_mp, chunk),
        out_shape=jax.ShapeDtypeStruct((rows, cols), BF16),
        in_specs=[any_spec, any_spec, any_spec, vmem_spec, vmem_spec, any_spec],
        out_specs=any_spec,
        scratch_shapes=[
            pltpu.VMEM((rows, width), BF16), pltpu.VMEM((rows, width), BF16), pltpu.VMEM((rows, width), BF16),
            pltpu.VMEM(out_weight.shape, BF16),
            pltpu.VMEM((rows, HEAD), F32),
            pltpu.VMEM((rows, rows), BF16),
            pltpu.VMEM((n_ctx, width + 8, HEAD), F32),
            pltpu.VMEM((width, 2 * HEAD), BF16),
            pltpu.VMEM((n_mp, rows, width), BF16),
            pltpu.VMEM((rows, cols), BF16),
            dma((4,)), dma((n_chunk,)), dma((n_ctx - 1,)), dma((n_ctx - 1,)),
            dma((n_mp - 1, n_chunk)), dma((n_mp - 1, n_chunk)),
        ],
        compiler_params=pltpu.CompilerParams(collective_id=0, has_side_effects=True, vmem_limit_bytes=56 << 20),
        cost_estimate=pl.CostEstimate(flops=7 * 10**9, bytes_accessed=9 << 20, transcendentals=1 << 20),
    )(queries, keys, values, segment_ids.reshape(1, rows), norm_gain.reshape(1, width), out_weight)


def solution(mesh):
    in_specs = (
        P(("dp", "ctx"), "mp"),
        P(("dp", "ctx"), "mp"),
        P(("dp", "ctx"), "mp"),
        P(("dp", "ctx")),
        P("mp"),
        P(None, "mp"),
    )
    out_specs = P(("dp", "ctx"), "mp")
    return jax.shard_map(
        per_device, mesh=mesh, in_specs=in_specs, out_specs=out_specs, check_vma=False
    )
```

time: 133 us -> 103 us (0.77)
  the two profiles are of different devices: /device:TPU:0 before, /device:TPU:8 now
where the time goes in v1:
time: 103 us
  Pallas kernels  100 us (97%)
  local copies, waits for them, and re-layouts  3.08 us (3%)
    pallas_call x1, Pallas kernels, per_device(): pl.pallas_call(functools.partial(kernel, n_ctx, n_mp, chunk), out_shape=j...  100 us
    unnamed x1, local copies, waits for them, and re-layouts  3.08 us

profile of v1, /device:TPU:8, one launch (start us, length us, event | category | flops | bytes accessed | tf_op | source)
XLA Modules:
  0.0 103.2 jit_solution(208710285770716982)
XLA Ops:
  0.0 100.1 %shard_map.64 = bf16[1024,1024]{1,0:T(8,128)(2,1)} custom-call(bf16[1024,512]{1,0:T(8,128)(2,1)} %q_hbm.1, bf16[1024,512]{1,0:T(8,128)(2,1)} %k_hbm.1, bf16[1024,512]{1,0:T(8,128)(2,1)} %v_hbm.1, s32[1,1024]{1,0:T(1,128)} %bitcast.2, f32[1,512]{1,0:T(1,128)} %bitcast.3, bf16[2048,1024]{1,0:T(8,128)(2,1)} %w_hbm.1), custom_call_target="tpu_custom_call" | custom-call | flops 7000000000 | bytes 9437184 | tf_op jit(solution)/shard_map/pallas_call | solution.py:142
  100.1 3.1 %copy.8 = bf16[1024,1024]{1,0:T(8,128)(2,1)} copy(bf16[1024,1024]{1,0:T(8,128)(2,1)} %shard_map.64) | data formatting | bytes 4194304

commit v2 on v1

--- a/solution.py
+++ b/solution.py
@@ -29,7 +29,7 @@
     return lax.dot_general(a, b, (((0,), (0,)), ((), ())), preferred_element_type=F32)
 
 
-def kernel(n_ctx, n_mp, chunk, q_hbm, k_hbm, v_hbm, seg_ref, gain_ref, w_hbm, out_hbm,
+def kernel(n_ctx, n_mp, chunk, piece, q_hbm, k_hbm, v_hbm, seg_ref, gain_ref, w_hbm, out_hbm,
            q, k, v, w, seg_col, mask, state, carry, hid, out_buf,
            load_sem, out_sem, st_send, st_recv, h_send, h_recv):
     ctx, mp = lax.axis_index("ctx"), lax.axis_index("mp")
@@ -90,7 +90,19 @@
     carry[:, 0:HEAD] = hi
     carry[:, HEAD:2 * HEAD] = (total - hi.astype(F32)).astype(BF16)
 
-    h_copies = []
+    pair = mp + 1 - 2 * lax.rem(mp, 2)
+    across = n_mp - 1 - mp
+    beside = across + 1 - 2 * lax.rem(across, 2)
+    is_end = (mp == 0) | (mp == n_mp - 1)
+    inner = jnp.logical_not(is_end)
+
+    def move(slot, c, way, lane, target):
+        part = hid.at[slot, pl.ds(c * piece, piece)]
+        return pltpu.make_async_remote_copy(
+            src_ref=part, dst_ref=part, send_sem=h_send.at[way, c], recv_sem=h_recv.at[lane, c],
+            device_id={"mp": target}, device_id_type=MESH)
+
+    per = chunk // piece
     for i in range(n_chunk):
         r0, r1 = i * chunk, (i + 1) * chunk
         on = (seg_col[r0:r1, :] == first).astype(F32)
@@ -103,44 +115,69 @@
             numer = inside + on * (both[:, 0:HEAD] + both[:, HEAD:2 * HEAD])
             mean = jnp.mean(numer * numer, axis=-1, keepdims=True)
             hid[mp, r0:r1, cols] = (numer * lax.rsqrt(mean + 1e-6) * gain_ref[:, cols]).astype(BF16)
-        for d in range(1, n_mp):
-            c = pltpu.make_async_remote_copy(
-                src_ref=hid.at[mp, pl.ds(r0, chunk)], dst_ref=hid.at[mp, pl.ds(r0, chunk)],
-                send_sem=h_send.at[d - 1, i], recv_sem=h_recv.at[d - 1, i],
-                device_id={"mp": lax.rem(mp + d, n_mp)}, device_id_type=MESH)
-            c.start()
-            h_copies.append(c)
+        for c in range(i * per, (i + 1) * per):
+            move(mp, c, 0, 0, pair).start()
+
+            @pl.when(inner)
+            def _():
+                move(mp, c, 1, 1, across).start()
 
     loads[3].wait()
-    outs = []
-    for i in range(n_chunk):
-        r0, r1 = i * chunk, (i + 1) * chunk
-        for d in range(1, n_mp):
-            h_copies[i * (n_mp - 1) + d - 1].wait_recv()
-        acc = nn(hid[0, r0:r1, :], w[0:width, :])
+
+    def project(c):
+        r0 = c * piece
+        acc = nn(hid[0, pl.ds(r0, piece), :], w[0:width, :])
         for p in range(1, n_mp):
-            acc = acc + nn(hid[p, r0:r1, :], w[p * width:(p + 1) * width, :])
-        out_buf[r0:r1, :] = acc.astype(BF16)
-        c = pltpu.make_async_copy(out_buf.at[pl.ds(r0, chunk)], out_hbm.at[pl.ds(r0, chunk)], out_sem.at[i])
-        c.start()
-        outs.append(c)
-    for c in h_copies:
-        c.wait_send()
-    for c in outs:
-        c.wait()
+            acc = acc + nn(hid[p, pl.ds(r0, piece), :], w[p * width:(p + 1) * width, :])
+        out_buf[pl.ds(r0, piece), :] = acc.astype(BF16)
+        pltpu.make_async_copy(out_buf.at[pl.ds(r0, piece)], out_hbm.at[pl.ds(r0, piece)], out_sem.at[c]).start()
+
+    n_piece = rows // piece
+
+    @pl.loop(0, n_piece)
+    def _(c):
+        move(pair, c, 0, 0, pair).wait_recv()
+
+        @pl.when(inner)
+        def _():
+            move(pair, c, 2, 2, across).start()
+        move(across, c, 0, 1, pair).wait_recv()
+
+        @pl.when(inner)
+        def _():
+            move(across, c, 3, 1, pair).start()
+        move(beside, c, 0, 2, pair).wait_recv()
+
+        @pl.when(inner)
+        def _():
+            move(beside, c, 4, 2, pair).start()
+        project(c)
+
+    @pl.loop(0, n_piece)
+    def _(c):
+        move(mp, c, 0, 0, pair).wait_send()
+
+        @pl.when(inner)
+        def _():
+            move(mp, c, 1, 1, across).wait_send()
+            move(pair, c, 2, 2, across).wait_send()
+            move(across, c, 3, 1, pair).wait_send()
+            move(beside, c, 4, 2, pair).wait_send()
+        pltpu.make_async_copy(
+            out_buf.at[pl.ds(c * piece, piece)], out_hbm.at[pl.ds(c * piece, piece)], out_sem.at[c]).wait()
 
 
 def per_device(queries, keys, values, segment_ids, norm_gain, out_weight):
     n_ctx, n_mp = lax.axis_size("ctx"), lax.axis_size("mp")
     rows, width = queries.shape
     cols = out_weight.shape[1]
-    chunk = 256
-    n_chunk = rows // chunk
+    chunk, piece = 256, 128
+    n_piece = rows // piece
     any_spec = pl.BlockSpec(memory_space=pl.ANY)
     vmem_spec = pl.BlockSpec(memory_space=pltpu.VMEM)
     dma = pltpu.SemaphoreType.DMA
     return pl.pallas_call(
-        functools.partial(kernel, n_ctx, n_mp, chunk),
+        functools.partial(kernel, n_ctx, n_mp, chunk, piece),
         out_shape=jax.ShapeDtypeStruct((rows, cols), BF16),
         in_specs=[any_spec, any_spec, any_spec, vmem_spec, vmem_spec, any_spec],
         out_specs=any_spec,
@@ -153,8 +190,8 @@
             pltpu.VMEM((width, 2 * HEAD), BF16),
             pltpu.VMEM((n_mp, rows, width), BF16),
             pltpu.VMEM((rows, cols), BF16),
-            dma((4,)), dma((n_chunk,)), dma((n_ctx - 1,)), dma((n_ctx - 1,)),
-            dma((n_mp - 1, n_chunk)), dma((n_mp - 1, n_chunk)),
+            dma((4,)), dma((n_piece,)), dma((n_ctx - 1,)), dma((n_ctx - 1,)),
+            dma((5, n_piece)), dma((3, n_piece)),
         ],
         compiler_params=pltpu.CompilerParams(collective_id=0, has_side_effects=True, vmem_limit_bytes=56 << 20),
         cost_estimate=pl.CostEstimate(flops=7 * 10**9, bytes_accessed=9 << 20, transcendentals=1 << 20),

time: 103 us -> 84.2 us (0.82)
  the two profiles are of different devices: /device:TPU:8 before, /device:TPU:0 now
where the time goes in v2:
time: 84.2 us; the launch traced here: 84 us
  Pallas kernels  80.9 us (96%)
  local copies, waits for them, and re-layouts  3.08 us (4%)
    pallas_call x1, Pallas kernels, per_device(): pl.pallas_call(functools.partial(kernel, n_ctx, n_mp, chunk, piece), out_...  80.9 us
    unnamed x1, local copies, waits for them, and re-layouts  3.08 us

profile of v2, /device:TPU:0, one launch (start us, length us, event | category | flops | bytes accessed | tf_op | source)
XLA Modules:
  0.0 84.0 jit_solution(5126931739977900882)
XLA Ops:
  0.0 80.9 %shard_map.64 = bf16[1024,1024]{1,0:T(8,128)(2,1)} custom-call(bf16[1024,512]{1,0:T(8,128)(2,1)} %q_hbm.1, bf16[1024,512]{1,0:T(8,128)(2,1)} %k_hbm.1, bf16[1024,512]{1,0:T(8,128)(2,1)} %v_hbm.1, s32[1,1024]{1,0:T(1,128)} %bitcast.2, f32[1,512]{1,0:T(1,128)} %bitcast.3, bf16[2048,1024]{1,0:T(8,128)(2,1)} %w_hbm.1), custom_call_target="tpu_custom_call" | custom-call | flops 7000000000 | bytes 9437184 | tf_op jit(solution)/shard_map/pallas_call | solution.py:179
  80.9 3.1 %copy.8 = bf16[1024,1024]{1,0:T(8,128)(2,1)} copy(bf16[1024,1024]{1,0:T(8,128)(2,1)} %shard_map.64) | data formatting | bytes 4194304

commit v3 on v2

--- a/solution.py
+++ b/solution.py
@@ -29,9 +29,10 @@
     return lax.dot_general(a, b, (((0,), (0,)), ((), ())), preferred_element_type=F32)
 
 
-def kernel(n_ctx, n_mp, chunk, piece, q_hbm, k_hbm, v_hbm, seg_ref, gain_ref, w_hbm, out_hbm,
+def kernel(n_ctx, n_mp, chunk, piece, whole, ahead, q_hbm, k_hbm, v_hbm, seg_ref, gain_ref, w_hbm, out_hbm,
            q, k, v, w, seg_col, mask, state, carry, hid, out_buf,
-           load_sem, out_sem, st_send, st_recv, h_send, h_recv):
+           wx, part, load_sem, out_sem, st_send, st_recv, h_send, h_recv,
+           w_send, w_recv, p_send, p_recv):
     ctx, mp = lax.axis_index("ctx"), lax.axis_index("mp")
     rows, width = q.shape
     heads = width // HEAD
@@ -47,6 +48,20 @@
     for d in range(1, n_ctx):
         pl.semaphore_signal(barrier, inc=1, device_id={"ctx": lax.rem(ctx + d, n_ctx)}, device_id_type=MESH)
 
+    dp = lax.axis_index("dp")
+    flip = lambda i: i + 1 - 2 * lax.rem(i, 2)
+    dp_near, dp_far, twin = flip(dp), lax.rem(dp + 2, 4), flip(ctx)
+    for other in (dp_near, dp_far):
+        pl.semaphore_signal(barrier, inc=1, device_id={"dp": other}, device_id_type=MESH)
+    pair = flip(mp)
+    across = n_mp - 1 - mp
+    beside = flip(across)
+    is_end = (mp == 0) | (mp == n_mp - 1)
+    inner = jnp.logical_not(is_end)
+    low = lax.rem(ctx, 2)
+    mine = dp * 2 + low
+    strip = wx.shape[2]
+
     seg_row = seg_ref[...].astype(F32)
     seg_col[...] = jnp.transpose(jnp.broadcast_to(seg_row, (HEAD, rows)))
     first = seg_col[0:1, :]
@@ -60,7 +75,28 @@
         cols = slice(h * HEAD, (h + 1) * HEAD)
         state[ctx, h * HEAD:(h + 1) * HEAD, :] = tn(k[:, cols] * in_final, v[:, cols])
     state[ctx, width:width + 8, :] = jnp.broadcast_to(last, (8, HEAD))
-    pl.semaphore_wait(barrier, n_mp - 1 + n_ctx - 1)
+    pl.semaphore_wait(barrier, n_mp - 1 + n_ctx - 1 + 2)
+
+    def lend(n, block):
+        return pltpu.make_async_remote_copy(
+            src_ref=w_hbm.at[pl.ds(pl.multiple_of(block * width + mine * strip, strip), strip)], dst_ref=wx.at[mine, n],
+            send_sem=w_send.at[n], recv_sem=w_recv.at[n], device_id={"mp": pair}, device_id_type=MESH)
+
+    def share(g, n, to):
+        return pltpu.make_async_remote_copy(
+            src_ref=wx.at[g], dst_ref=wx.at[g], send_sem=w_send.at[n], recv_sem=w_recv.at[n],
+            device_id=to, device_id_type=MESH)
+
+    near, far, core = {"dp": dp_near}, {"dp": dp_far}, {"ctx": twin}
+    got = (mine, dp_near * 2 + low, dp_far * 2 + low, flip(dp_far) * 2 + low)
+    lent = [lend(n, block) for n, block in enumerate((pair, beside, across))]
+    shares = [share(got[0], 3, near), share(got[0], 4, far), share(got[1], 5, far)] + [
+        share(got[j], 6 + j, core) for j in range(4)]
+
+    @pl.when(is_end)
+    def _():
+        for c in lent:
+            c.start()
     st_copies = []
     for d in range(1, n_ctx):
         c = pltpu.make_async_remote_copy(
@@ -89,12 +125,6 @@
     hi = total.astype(BF16)
     carry[:, 0:HEAD] = hi
     carry[:, HEAD:2 * HEAD] = (total - hi.astype(F32)).astype(BF16)
-
-    pair = mp + 1 - 2 * lax.rem(mp, 2)
-    across = n_mp - 1 - mp
-    beside = across + 1 - 2 * lax.rem(across, 2)
-    is_end = (mp == 0) | (mp == n_mp - 1)
-    inner = jnp.logical_not(is_end)
 
     def move(slot, c, way, lane, target):
         part = hid.at[slot, pl.ds(c * piece, piece)]
@@ -116,53 +146,106 @@
             mean = jnp.mean(numer * numer, axis=-1, keepdims=True)
             hid[mp, r0:r1, cols] = (numer * lax.rsqrt(mean + 1e-6) * gain_ref[:, cols]).astype(BF16)
         for c in range(i * per, (i + 1) * per):
-            move(mp, c, 0, 0, pair).start()
-
-            @pl.when(inner)
+            @pl.when(is_end | (c in whole))
             def _():
-                move(mp, c, 1, 1, across).start()
+                move(mp, c, 0, 0, pair).start()
+
+            if c < ahead:
+                @pl.when(inner)
+                def _():
+                    move(mp, c, 1, 1, across).start()
 
     loads[3].wait()
+    n_piece = rows // piece
+
+    def store(c, acc):
+        r0 = c * piece
+        out_buf[r0:r0 + piece, :] = acc.astype(BF16)
+        pltpu.make_async_copy(out_buf.at[pl.ds(r0, piece)], out_hbm.at[pl.ds(r0, piece)], out_sem.at[c]).start()
 
     def project(c):
         r0 = c * piece
-        acc = nn(hid[0, pl.ds(r0, piece), :], w[0:width, :])
+        acc = nn(hid[0, r0:r0 + piece, :], w[0:width, :])
         for p in range(1, n_mp):
-            acc = acc + nn(hid[p, pl.ds(r0, piece), :], w[p * width:(p + 1) * width, :])
-        out_buf[pl.ds(r0, piece), :] = acc.astype(BF16)
-        pltpu.make_async_copy(out_buf.at[pl.ds(r0, piece)], out_hbm.at[pl.ds(r0, piece)], out_sem.at[c]).start()
-
-    n_piece = rows // piece
-
-    @pl.loop(0, n_piece)
-    def _(c):
-        move(pair, c, 0, 0, pair).wait_recv()
-
-        @pl.when(inner)
-        def _():
-            move(pair, c, 2, 2, across).start()
-        move(across, c, 0, 1, pair).wait_recv()
-
-        @pl.when(inner)
-        def _():
-            move(across, c, 3, 1, pair).start()
-        move(beside, c, 0, 2, pair).wait_recv()
-
-        @pl.when(inner)
-        def _():
-            move(beside, c, 4, 2, pair).start()
-        project(c)
-
-    @pl.loop(0, n_piece)
-    def _(c):
-        move(mp, c, 0, 0, pair).wait_send()
-
-        @pl.when(inner)
-        def _():
+            acc = acc + nn(hid[p, r0:r0 + piece, :], w[p * width:(p + 1) * width, :])
+        store(c, acc)
+
+    def hand(c):
+        return pltpu.make_async_remote_copy(
+            src_ref=part.at[c], dst_ref=part.at[c], send_sem=p_send.at[c], recv_sem=p_recv.at[c],
+            device_id={"mp": pair}, device_id_type=MESH)
+
+    @pl.when(inner)
+    def _():
+        for c in lent:
+            c.wait_recv()
+        for n in (0, 1, 3):
+            shares[n].start()
+        move(pair, 0, 0, 0, pair).wait_recv()
+        move(pair, 0, 2, 2, across).start()
+        for c in range(n_piece):
+            if c + 1 < n_piece:
+                move(pair, c + 1, 0, 0, pair).wait_recv()
+                move(pair, c + 1, 2, 2, across).start()
+            if c + ahead < n_piece:
+                move(mp, c + ahead, 1, 1, across).start()
+            if c == 1:
+                shares[0].wait_recv()
+                shares[2].start()
+                shares[4].start()
+                shares[1].wait_recv()
+                shares[5].start()
+            if c == 2:
+                shares[2].wait_recv()
+                shares[6].start()
+            move(across, c, 0, 1, pair).wait_recv()
+            if c in whole:
+                move(across, c, 3, 1, pair).start()
+            move(beside, c, 0, 2, pair).wait_recv()
+            if c in whole:
+                move(beside, c, 4, 2, pair).start()
+            else:
+                if c == 2:
+                    for n in range(3, 7):
+                        shares[n].wait_recv()
+                r0 = c * piece
+                acc = None
+                for n, slot in enumerate((mp, across, beside)):
+                    term = nn(hid[slot, r0:r0 + piece, :], wx[:, n].reshape(width, -1))
+                    acc = term if acc is None else acc + term
+                part[c] = acc.astype(BF16)
+                hand(c).start()
+            project(c)
+        for c in range(n_piece):
             move(mp, c, 1, 1, across).wait_send()
             move(pair, c, 2, 2, across).wait_send()
-            move(across, c, 3, 1, pair).wait_send()
-            move(beside, c, 4, 2, pair).wait_send()
+            if c in whole:
+                move(mp, c, 0, 0, pair).wait_send()
+                move(across, c, 3, 1, pair).wait_send()
+                move(beside, c, 4, 2, pair).wait_send()
+            else:
+                hand(c).wait_send()
+        for c in shares:
+            c.wait_send()
+
+    @pl.when(is_end)
+    def _():
+        for c in range(n_piece):
+            if c in whole:
+                for lane in range(3):
+                    move(across, c, 0, lane, pair).wait_recv()
+                project(c)
+            else:
+                r0 = c * piece
+                own = nn(hid[mp, r0:r0 + piece, :], w[pl.ds(pl.multiple_of(mp * width, width), width), :])
+                hand(c).wait_recv()
+                store(c, own + part[c].astype(F32))
+        for c in range(n_piece):
+            move(mp, c, 0, 0, pair).wait_send()
+        for c in lent:
+            c.wait_send()
+
+    for c in range(n_piece):
         pltpu.make_async_copy(
             out_buf.at[pl.ds(c * piece, piece)], out_hbm.at[pl.ds(c * piece, piece)], out_sem.at[c]).wait()
 
@@ -173,11 +256,13 @@
     cols = out_weight.shape[1]
     chunk, piece = 256, 128
     n_piece = rows // piece
+    whole, ahead = (0, 1, n_piece - 1), 2
+    group = 8
     any_spec = pl.BlockSpec(memory_space=pl.ANY)
     vmem_spec = pl.BlockSpec(memory_space=pltpu.VMEM)
     dma = pltpu.SemaphoreType.DMA
     return pl.pallas_call(
-        functools.partial(kernel, n_ctx, n_mp, chunk, piece),
+        functools.partial(kernel, n_ctx, n_mp, chunk, piece, whole, ahead),
         out_shape=jax.ShapeDtypeStruct((rows, cols), BF16),
         in_specs=[any_spec, any_spec, any_spec, vmem_spec, vmem_spec, any_spec],
         out_specs=any_spec,
@@ -190,8 +275,11 @@
             pltpu.VMEM((width, 2 * HEAD), BF16),
             pltpu.VMEM((n_mp, rows, width), BF16),
             pltpu.VMEM((rows, cols), BF16),
+            pltpu.VMEM((group, n_mp - 1, width // group, cols), BF16),
+            pltpu.VMEM((n_piece, piece, cols), BF16),
             dma((4,)), dma((n_piece,)), dma((n_ctx - 1,)), dma((n_ctx - 1,)),
             dma((5, n_piece)), dma((3, n_piece)),
+            dma((10,)), dma((10,)), dma((n_piece,)), dma((n_piece,)),
         ],
         compiler_params=pltpu.CompilerParams(collective_id=0, has_side_effects=True, vmem_limit_bytes=56 << 20),
         cost_estimate=pl.CostEstimate(flops=7 * 10**9, bytes_accessed=9 << 20, transcendentals=1 << 20),

time: 84.2 us -> 76.5 us (0.909)
  Pallas kernels: 80.9 us -> 73.2 us
    pallas_call x1, Pallas kernels: 80.9 us -> 73.2 us  [per_device(): pl.pallas_call(functools.partial(kernel, n_ctx, n_mp, chunk, piece, whole...]
where the time goes in v3:
time: 76.5 us; the launch traced here: 76.3 us
  Pallas kernels  73.2 us (96%)
  local copies, waits for them, and re-layouts  3.08 us (4%)
    pallas_call x1, Pallas kernels, per_device(): pl.pallas_call(functools.partial(kernel, n_ctx, n_mp, chunk, piece, whole...  73.2 us
    unnamed x1, local copies, waits for them, and re-layouts  3.08 us

profile of v3, /device:TPU:0, one launch (start us, length us, event | category | flops | bytes accessed | tf_op | source)
XLA Modules:
  0.0 76.3 jit_solution(9139138517625786419)
XLA Ops:
  0.0 73.2 %shard_map.64 = bf16[1024,1024]{1,0:T(8,128)(2,1)} custom-call(bf16[1024,512]{1,0:T(8,128)(2,1)} %q_hbm.1, bf16[1024,512]{1,0:T(8,128)(2,1)} %k_hbm.1, bf16[1024,512]{1,0:T(8,128)(2,1)} %v_hbm.1, s32[1,1024]{1,0:T(1,128)} %bitcast.2, f32[1,512]{1,0:T(1,128)} %bitcast.3, bf16[2048,1024]{1,0:T(8,128)(2,1)} %w_hbm.1), custom_call_target="tpu_custom_call" | custom-call | flops 7000000000 | bytes 9437184 | tf_op jit(solution)/shard_map/pallas_call | solution.py:264
  73.2 3.1 %copy.8 = bf16[1024,1024]{1,0:T(8,128)(2,1)} copy(bf16[1024,1024]{1,0:T(8,128)(2,1)} %shard_map.64) | data formatting | bytes 4194304

commit v4 on v3

--- a/solution.py
+++ b/solution.py
@@ -205,7 +205,7 @@
             if c in whole:
                 move(beside, c, 4, 2, pair).start()
             else:
-                if c == 2:
+                if c == whole.index(n_piece - 1):
                     for n in range(3, 7):
                         shares[n].wait_recv()
                 r0 = c * piece
@@ -256,7 +256,7 @@
     cols = out_weight.shape[1]
     chunk, piece = 256, 128
     n_piece = rows // piece
-    whole, ahead = (0, 1, n_piece - 1), 2
+    whole, ahead = (0, 1, 2, n_piece - 1), 4
     group = 8
     any_spec = pl.BlockSpec(memory_space=pl.ANY)
     vmem_spec = pl.BlockSpec(memory_space=pltpu.VMEM)

time: 76.5 us -> 73.7 us (0.963)
  Pallas kernels: 73.2 us -> 70.4 us
    pallas_call x1, Pallas kernels: 73.2 us -> 70.4 us  [per_device(): pl.pallas_call(functools.partial(kernel, n_ctx, n_mp, chunk, piece, whole...]
where the time goes in v4:
time: 73.7 us; the launch traced here: 73.5 us
  Pallas kernels  70.4 us (96%)
  local copies, waits for them, and re-layouts  3.08 us (4%)
    pallas_call x1, Pallas kernels, per_device(): pl.pallas_call(functools.partial(kernel, n_ctx, n_mp, chunk, piece, whole...  70.4 us
    unnamed x1, local copies, waits for them, and re-layouts  3.08 us

profile of v4, /device:TPU:0, one launch (start us, length us, event | category | flops | bytes accessed | tf_op | source)
XLA Modules:
  0.0 73.5 jit_solution(7418757967326523244)
XLA Ops:
  0.0 70.4 %shard_map.64 = bf16[1024,1024]{1,0:T(8,128)(2,1)} custom-call(bf16[1024,512]{1,0:T(8,128)(2,1)} %q_hbm.1, bf16[1024,512]{1,0:T(8,128)(2,1)} %k_hbm.1, bf16[1024,512]{1,0:T(8,128)(2,1)} %v_hbm.1, s32[1,1024]{1,0:T(1,128)} %bitcast.2, f32[1,512]{1,0:T(1,128)} %bitcast.3, bf16[2048,1024]{1,0:T(8,128)(2,1)} %w_hbm.1), custom_call_target="tpu_custom_call" | custom-call | flops 7000000000 | bytes 9437184 | tf_op jit(solution)/shard_map/pallas_call | solution.py:264
  70.4 3.1 %copy.8 = bf16[1024,1024]{1,0:T(8,128)(2,1)} copy(bf16[1024,1024]{1,0:T(8,128)(2,1)} %shard_map.64) | data formatting | bytes 4194304
